TPU v7x, 512 devices: a whole 4x4x16 slice. The times are simulated.
512 devices in a mesh: dp: 16 (over z), expert: 32 (over y, x, core).
Axes of the slice: x: 4, y: 4, z: 16, core: 2. Of those that a mesh axis runs over, the one named last changes fastest.
Arguments:
- tokens: bfloat16 [65536, 1024], P(('dp', 'expert')), may hold values from -6 to 6
- grad_out: bfloat16 [65536, 1024], P(('dp', 'expert')), may hold values from -6 to 6
- expert_ids: int32 [65536, 2], P(('dp', 'expert')), may hold values from 0 to 31, all different within a row; in each aligned block of 128 rows (0 to 127, 128 to 255, ...) at most 16 rows name the same one
- route_probs: bfloat16 [65536, 2], P(('dp', 'expert')), may hold values from 0.19921875 to 1
- gate_up_weight: bfloat16 [1024, 32, 1536], P('dp', 'expert'), may hold values from -0.1875 to 0.1875
- down_weight: bfloat16 [32, 768, 1024], P('expert'), may hold values from -0.21875 to 0.21875
- gate_up_scale_index: int32 [8, 32, 2], P(None, 'expert'), may hold values from 0 to 15
- down_scale_index: int32 [32, 6], P('expert'), may hold values from 0 to 15
- scale_table: float32 [16], replicated, may hold values from 0.5 to 2
Outputs:
- token_grad: bfloat16 [65536, 1024], P(('dp', 'expert'))
- prob_grad: float32 [65536, 2], P(('dp', 'expert'))
- gate_up_grad: bfloat16 [1024, 32, 1536], P('dp', 'expert')
- down_grad: bfloat16 [32, 768, 1024], P('expert')
Inputs may be any that keep to these rules, and one draw needn't show every extreme that they name: `expert_ids`: each row names two different experts. The 128 rows of one device name one expert at most 16 times, and in every draw some device's rows name some expert exactly 16 times.
All inputs are finite; a program needn't handle non-finite values.
Results may differ from a plain program's by a relative error of at most 0.022.
Values may be sent and summed in bfloat16 or wider, within the bound.
No kernel may reach another device: no remote copies, remote signals or barrier semaphores. Data moves between devices by JAX's collectives and lax.ppermute only.
A program may use at most 64 MiB of HBM per device.

v0:
```python
import jax
import jax.numpy as jnp
from jax import lax
from jax.sharding import PartitionSpec as P

QBLOCK = 128


def lookup(level_index, level_table):
    onehot = (level_index[..., None] == jnp.arange(level_table.shape[0], dtype=jnp.int32)).astype(
        level_table.dtype
    )
    return jnp.sum(onehot * level_table, axis=-1)


def slot_tables(routes, experts, capacity):
    flat_routes = routes.reshape(-1)
    expert_hits = (flat_routes[:, None] == jnp.arange(experts, dtype=jnp.int32)[None, :]).astype(
        jnp.int32
    )
    place = jnp.arange(flat_routes.shape[0], dtype=jnp.int32)
    earlier = (place[None, :] < place[:, None]).astype(jnp.bfloat16)
    before = jnp.dot(
        earlier, expert_hits.astype(jnp.bfloat16), preferred_element_type=jnp.float32
    ).astype(jnp.int32)
    slot_rank = jnp.sum(before * expert_hits, axis=1)
    destination = flat_routes * capacity + slot_rank
    table_hits = destination[:, None] == jnp.arange(experts * capacity, dtype=jnp.int32)[None, :]
    return table_hits.astype(jnp.float32).reshape(routes.shape[0], 2, experts * capacity)


def body(
    tokens,
    grad_out,
    expert_ids,
    route_probs,
    gate_up_weight,
    down_weight,
    gate_up_scale_index,
    down_scale_index,
    scale_table,
):
    high = lax.Precision.HIGHEST
    f32 = jnp.float32
    groups = lax.axis_size("expert")
    tok_dev = tokens.shape[0]
    model_width = tokens.shape[1]
    per_device = down_weight.shape[0]
    hidden = down_weight.shape[1]
    experts = per_device * groups
    capacity = 4 * tok_dev // experts
    slots_all = experts * capacity
    slot_hits = slot_tables(expert_ids, experts, capacity)
    either = (slot_hits[:, 0] + slot_hits[:, 1]).astype(jnp.bfloat16)
    row_shape = (groups, per_device, capacity, model_width)
    send_tokens = (
        jnp.einsum("ts,td->sd", either, tokens, preferred_element_type=f32)
        .astype(jnp.bfloat16)
        .reshape(row_shape)
    )
    send_grads = (
        jnp.einsum("ts,td->sd", either, grad_out, preferred_element_type=f32)
        .astype(jnp.bfloat16)
        .reshape(row_shape)
    )
    send_probs = (
        jnp.einsum("tks,tk->s", slot_hits, route_probs.astype(f32), precision=high)
        .astype(jnp.bfloat16)
        .reshape(row_shape[:3])
    )
    recv_tokens, recv_grads, recv_probs = (
        lax.all_to_all(send_tokens, "expert", split_axis=0, concat_axis=0, tiled=True),
        lax.all_to_all(send_grads, "expert", split_axis=0, concat_axis=0, tiled=True),
        lax.all_to_all(send_probs, "expert", split_axis=0, concat_axis=0, tiled=True),
    )
    level_rows = jnp.repeat(lookup(gate_up_scale_index, scale_table), QBLOCK, axis=0)
    full_scale = jnp.repeat(level_rows, hidden, axis=2)
    down_scale = jnp.repeat(lookup(down_scale_index, scale_table), QBLOCK, axis=1)
    down_eff = (down_weight.astype(f32) * down_scale[:, :, None]).astype(jnp.bfloat16)
    gathered = lax.all_gather(gate_up_weight, "dp", axis=0, tiled=True)
    gate_up_eff = (gathered.astype(f32) * full_scale).astype(jnp.bfloat16)
    projected = jnp.einsum("sjcd,djf->sjcf", recv_tokens, gate_up_eff, preferred_element_type=f32)
    gate_part = projected[..., :hidden]
    up_part = projected[..., hidden:]
    sigmoid_gate = jax.nn.sigmoid(gate_part)
    activated = gate_part * sigmoid_gate
    hidden_rows = (activated * up_part).astype(jnp.bfloat16)
    hidden_grad = jnp.einsum("sjcd,jfd->sjcf", recv_grads, down_eff, preferred_element_type=f32)
    probs_wide = recv_probs.astype(f32)[..., None]
    scaled_grad = probs_wide * hidden_grad
    gate_grad = scaled_grad * up_part * sigmoid_gate * (1.0 + gate_part * (1.0 - sigmoid_gate))
    up_grad = scaled_grad * activated
    joint_grad = jnp.concatenate([gate_grad, up_grad], axis=-1).astype(jnp.bfloat16)
    row_grads = jnp.einsum(
        "sjcf,djf->sjcd", joint_grad, gate_up_eff, preferred_element_type=f32
    ).astype(jnp.bfloat16)
    back_rows = lax.all_to_all(row_grads, "expert", split_axis=0, concat_axis=0, tiled=True)
    token_grad = jnp.dot(
        either, back_rows.reshape(slots_all, model_width), preferred_element_type=f32
    ).astype(jnp.bfloat16)
    expert_out = jnp.einsum("sjcf,jfd->sjcd", hidden_rows, down_eff, preferred_element_type=f32)
    back_out = lax.all_to_all(
        expert_out.astype(jnp.bfloat16), "expert", split_axis=0, concat_axis=0, tiled=True
    ).astype(expert_out.dtype)
    picked = jnp.einsum(
        "tks,sd->tkd", slot_hits, back_out.reshape(slots_all, model_width), precision=high
    )
    prob_grad = jnp.sum(picked * grad_out.astype(f32)[:, None, :], axis=-1)
    weighted = (probs_wide * hidden_rows.astype(f32)).astype(jnp.bfloat16)
    partial_sum = jnp.einsum("sjcd,sjcf->djf", recv_tokens, joint_grad, preferred_element_type=f32)
    gate_up_grad = lax.psum_scatter(
        (partial_sum * full_scale).astype(jnp.bfloat16), "dp", scatter_dimension=0, tiled=True
    )
    down_part = (
        jnp.einsum("sjcf,sjcd->jfd", weighted, recv_grads, preferred_element_type=f32)
        * down_scale[:, :, None]
    )
    down_grad = lax.psum(down_part.astype(jnp.bfloat16), "dp")
    return (token_grad, prob_grad, gate_up_grad, down_grad)


def solution(mesh):
    in_specs = (
        P(("dp", "expert"), None),
        P(("dp", "expert"), None),
        P(("dp", "expert"), None),
        P(("dp", "expert"), None),
        P("dp", "expert", None),
        P("expert", None, None),
        P(None, "expert", None),
        P("expert", None),
        P(),
    )
    out_specs = (
        P(("dp", "expert"), None),
        P(("dp", "expert"), None),
        P("dp", "expert", None),
        P("expert", None, None),
    )
    return jax.shard_map(body, mesh=mesh, in_specs=in_specs, out_specs=out_specs, check_vma=False)
```

profile of v0, /device:TPU:2, one launch (start us, length us, event | category | flops | bytes accessed | tf_op | source)
XLA Modules:
  0.0 353.9 jit_solution(2334480392853353179)
XLA Ops:
  7.2 0.7 all-gather.2.cloned.1.call-update
  7.9 0.8 copy.74
  8.8 0.2 fusion.16
  9.1 0.1 reduce_sum.39
  9.3 0.7 multiply_add_fusion
  10.0 0.9 fusion.34
  10.9 0.7 reshape.246
  11.6 9.4 %all-to-all-start = ((bf16[32,1,16]{2,1,0:T(2,128)(2,1)}), bf16[32,1,16]{2,1,0:T(2,128)(2,1)S(1)}, u32[]{:S(2)}, u32[]{:S(2)}) async-start(bf16[32,1,16]{2,1,0:T(2,128)(2,1)} %reshape.246), calls=%async_computation | async-start | bytes 32768 | tf_op jit(solution)/shard_map/all_to_all | solution.py:74
  21.2 1.4 convolution_convert_fusion.1
  22.6 4.5 %all-to-all-done = bf16[32,1,16]{2,1,0:T(2,128)(2,1)S(1)} async-done(((bf16[32,1,16]{2,1,0:T(2,128)(2,1)}), bf16[32,1,16]{2,1,0:T(2,128)(2,1)S(1)}, u32[]{:S(2)}, u32[]{:S(2)}) %all-to-all-start) | async-done | bytes 1056 | tf_op jit(solution)/shard_map/all_to_all | solution.py:74
  27.2 5.7 %all-to-all-start.2 = ((bf16[32,1,16,1024]{3,2,1,0:T(8,128)(2,1)}), bf16[32,1,16,1024]{3,2,1,0:T(8,128)(2,1)}, u32[]{:S(2)}, u32[]{:S(2)}) async-start(bf16[32,1,16,1024]{3,2,1,0:T(8,128)(2,1)} %bitcast.19), calls=%async_computation.2 | async-start | bytes 2097152 | tf_op jit(solution)/shard_map/all_to_all | solution.py:72
  32.9 0.2 select_reduce_fusion
  33.1 0.2 fusion.43
  33.3 0.7 broadcast_bitcast_fusion.1
  34.0 1.5 convolution_convert_fusion.2
  35.5 55.5 %all-gather.2.cloned.1.call-done = bf16[1024,1,1536]{2,0,1:T(8,128)(2,1)} async-done(((bf16[64,1,1536]{2,0,1:T(8,128)(2,1)}), bf16[1024,1,1536]{2,0,1:T(8,128)(2,1)}) %all-gather.2.cloned.1.call-update) | async-done | bytes 3145744 | tf_op jit(solution)/shard_map/all_gather | solution.py:80
  91.0 3.2 copy.76
  94.2 7.2 %all-to-all-start.1 = ((bf16[32,1,16,1024]{3,2,1,0:T(8,128)(2,1)}), bf16[32,1,16,1024]{3,2,1,0:T(8,128)(2,1)}, u32[]{:S(2)}, u32[]{:S(2)}) async-start(bf16[32,1,16,1024]{3,2,1,0:T(8,128)(2,1)} %bitcast.139), calls=%async_computation.1 | async-start | bytes 2097152 | tf_op jit(solution)/shard_map/all_to_all | solution.py:73
  101.5 0.2 reduce-scatter.4.cloned.1.call-start
  101.7 0.8 broadcast_in_dim.14
  102.5 1.2 fusion.3
  103.7 1.7 copy-done.1
  105.4 1.7 copy-done.2
  107.1 5.1 %convolution_bitcast_fusion = f32[32,1,16,1536]{3,0,2,1:T(8,128)} fusion(bf16[1024,1536,1]{0,1,2:T(8,128)(2,1)S(1)} %fusion.3, bf16[32,1,16,1024]{3,2,1,0:T(8,128)(2,1)} %all-to-all-done.2), kind=kOutput, calls=%fused_computation.4 | convolution fusion | flops 1610612736 | bytes 7340032 | tf_op jit(solution)/shard_map/sjcd,djf->sjcf/dot_general | solution.py:82
  112.2 5.5 %all-to-all-done.1 = bf16[32,1,16,1024]{3,2,1,0:T(8,128)(2,1)} async-done(((bf16[32,1,16,1024]{3,2,1,0:T(8,128)(2,1)}), bf16[32,1,16,1024]{3,2,1,0:T(8,128)(2,1)}, u32[]{:S(2)}, u32[]{:S(2)}) %all-to-all-start.1) | async-done | bytes 1048608 | tf_op jit(solution)/shard_map/all_to_all | solution.py:73
  117.6 5.3 %fusion.31 = (bf16[32,16,768]{2,0,1:T(8,128)(2,1)S(1)}, bf16[32,16,768]{2,0,1:T(8,128)(2,1)S(1)}, bf16[32,1,16,768]{3,0,2,1:T(8,128)(2,1)}) fusion(f32[32,1,16,1536]{3,0,2,1:T(8,128)} %convolution_bitcast_fusion, bf16[32,1,16,1024]{3,2,1,0:T(8,128)(2,1)} %all-to-all-done.1, bf16[1,768,1024]{2,1,0:T(8,128)(2,1)S(1)} %copy-done.11, f32[768]{0:T(1024)S(1)} %copy-done.8, ...), kind=kOutput, calls=%fused_computation.49 | convolution fusion | flops 813957120 | bytes 8131584 | tf_op jit(solution)/shard_map/sjcd,jfd->sjcf/dot_general | solution.py:88
  123.0 3.8 %fusion.17 = f32[1536,1024,1]{1,0,2:T(8,128)S(1)} fusion(bf16[32,16,768]{2,0,1:T(8,128)(2,1)S(1)} %get-tuple-element.25, bf16[32,16,768]{2,0,1:T(8,128)(2,1)S(1)} %get-tuple-element.24, bf16[32,1,16,1024]{3,2,1,0:T(8,128)(2,1)} %all-to-all-done.2), kind=kOutput, calls=%fused_computation.36 | convolution fusion | flops 1613758464 | bytes 8912896 | tf_op jit(solution)/shard_map/sjcd,sjcf->djf/dot_general | solution.py:110
  126.8 1.8 fusion.2
  128.6 3.0 copy.96
  131.6 1.4 copy-done.12
  133.0 0.2 copy-done.14
  133.2 1.1 fusion.12
  134.3 1.6 copy.86
  135.8 5.7 %all-to-all-start.4 = ((bf16[32,1,16,1024]{3,2,1,0:T(8,128)(2,1)}), bf16[32,1,16,1024]{3,2,1,0:T(8,128)(2,1)}, u32[]{:S(2)}, u32[]{:S(2)}) async-start(bf16[32,1,16,1024]{3,2,1,0:T(8,128)(2,1)} %copy.86), calls=%async_computation.4 | async-start | bytes 2097152 | tf_op jit(solution)/shard_map/all_to_all | solution.py:102
  141.6 0.3 all-reduce.2.cloned.1.call-start
  141.8 4.1 %fusion.11 = bf16[1,768,1024]{2,1,0:T(8,128)(2,1)} fusion(f32[768]{0:T(1024)S(1)} %copy-done.8, bf16[32,1,16,1024]{3,2,1,0:T(8,128)(2,1)} %all-to-all-done.1, bf16[32,1,16,768]{3,0,2,1:T(8,128)(2,1)} %get-tuple-element.26, f32[32,16]{0,1:T(8,128)S(1)} %copy.78), kind=kOutput, calls=%fused_computation.23 | convolution fusion | flops 808058880 | bytes 3412992 | tf_op jit(solution)/shard_map/sjcf,sjcd->jfd/dot_general | solution.py:115
  146.0 3.2 fusion.13
  149.2 1.6 copy.85
  150.7 7.1 %all-to-all-done.4 = bf16[32,1,16,1024]{3,2,1,0:T(8,128)(2,1)} async-done(((bf16[32,1,16,1024]{3,2,1,0:T(8,128)(2,1)}), bf16[32,1,16,1024]{3,2,1,0:T(8,128)(2,1)}, u32[]{:S(2)}, u32[]{:S(2)}) %all-to-all-start.4) | async-done | bytes 1048608 | tf_op jit(solution)/shard_map/all_to_all | solution.py:102
  157.8 5.0 %all-to-all-start.3 = ((bf16[32,1,16,1024]{3,2,1,0:T(8,128)(2,1)}), bf16[32,1,16,1024]{3,2,1,0:T(8,128)(2,1)S(1)}, u32[]{:S(2)}, u32[]{:S(2)}) async-start(bf16[32,1,16,1024]{3,2,1,0:T(8,128)(2,1)} %copy.85), calls=%async_computation.3 | async-start | bytes 2097152 | tf_op jit(solution)/shard_map/all_to_all | solution.py:97
  162.9 2.4 fusion.14
  165.3 13.8 %all-to-all-done.3 = bf16[32,1,16,1024]{3,2,1,0:T(8,128)(2,1)S(1)} async-done(((bf16[32,1,16,1024]{3,2,1,0:T(8,128)(2,1)}), bf16[32,1,16,1024]{3,2,1,0:T(8,128)(2,1)S(1)}, u32[]{:S(2)}, u32[]{:S(2)}) %all-to-all-start.3) | async-done | bytes 1048608 | tf_op jit(solution)/shard_map/all_to_all | solution.py:97
  179.1 1.0 convolution_convert_fusion.4
  180.1 22.4 %reduce-scatter.4.cloned.1.call-done = bf16[64,1536]{1,0:T(8,128)(2,1)} async-done(((bf16[1024,1536]{1,0:T(8,128)(2,1)}), bf16[64,1536]{1,0:T(8,128)(2,1)}) %reduce-scatter.4.cloned.1.call-update) | async-done | bytes 196624
  202.5 1.1 copy.97
  203.6 0.8 copy.88
  204.5 140.2 %all-reduce.2.cloned.1.call-done = bf16[1,768,1024]{2,1,0:T(8,128)(2,1)} async-done(((bf16[1,768,1024]{2,1,0:T(8,128)(2,1)}), bf16[1,768,1024]{2,1,0:T(8,128)(2,1)}) %all-reduce.2.cloned.1.call-update) | async-done | bytes 1572880 | tf_op jit(solution)/shard_map/psum | solution.py:118
  344.7 2.7 copy.122
  (49 shorter events, 0.7 us)
Async XLA Ops:
  7.2 14.0 %copy-start = (bf16[128,1024]{1,0:T(8,128)(2,1)S(1)}, bf16[128,1024]{1,0:T(8,128)(2,1)}, u32[]{:S(2)}) copy-start(bf16[128,1024]{1,0:T(8,128)(2,1)} %param.9) | copy-start | bytes 786436
  7.2 83.9 %all-gather.2.cloned.1.call-start = ((), (), s32[]{:S(2)}) async-start(), calls=%async_computation.6 | async-start | bytes 3342336 | tf_op jit(solution)/shard_map/all_gather | solution.py:80
  10.0 11.0 %copy-start.6 = (s32[128,2]{0,1:T(2,128)}, s32[128,2]{0,1:T(2,128)S(1)}, u32[]{:S(2)}) copy-start(s32[128,2]{0,1:T(2,128)S(1)} %multiply_add_fusion) | copy-start | bytes 3076
  11.6 15.6 %all-to-all-start = ((bf16[32,1,16]{2,1,0:T(2,128)(2,1)}), bf16[32,1,16]{2,1,0:T(2,128)(2,1)S(1)}, u32[]{:S(2)}, u32[]{:S(2)}) async-start(bf16[32,1,16]{2,1,0:T(2,128)(2,1)} %reshape.246), calls=%async_computation | async-start | bytes 32768 | tf_op jit(solution)/shard_map/all_to_all | solution.py:74
  21.1 11.8 %copy-start.9 = (s32[8,1,2]{0,2,1:T(2,128)S(1)}, s32[8,1,2]{0,2,1:T(2,128)}, u32[]{:S(2)}) copy-start(s32[8,1,2]{0,2,1:T(2,128)} %param.15) | copy-start | bytes 196
  21.1 11.8 %copy-start.10 = (f32[16]{0:T(128)S(1)}, f32[16]{0:T(128)}, u32[]{:S(2)}) copy-start(f32[16]{0:T(128)} %param.17) | copy-start | bytes 196
  21.1 12.0 %copy-start.13 = (s32[1,6]{1,0:T(1,128)S(1)}, s32[1,6]{1,0:T(1,128)}, u32[]{:S(2)}) copy-start(s32[1,6]{1,0:T(1,128)} %param.16) | copy-start | bytes 76
  21.2 12.9 %copy-start.4 = (bf16[128,1024]{1,0:T(8,128)(2,1)S(1)}, bf16[128,1024]{1,0:T(8,128)(2,1)}, u32[]{:S(2)}) copy-start(bf16[128,1024]{1,0:T(8,128)(2,1)} %param.10) | copy-start | bytes 786436
  27.2 67.1 %all-to-all-start.2 = ((bf16[32,1,16,1024]{3,2,1,0:T(8,128)(2,1)}), bf16[32,1,16,1024]{3,2,1,0:T(8,128)(2,1)}, u32[]{:S(2)}, u32[]{:S(2)}) async-start(bf16[32,1,16,1024]{3,2,1,0:T(8,128)(2,1)} %bitcast.19), calls=%async_computation.2 | async-start | bytes 2097152 | tf_op jit(solution)/shard_map/all_to_all | solution.py:72
  94.2 23.4 %all-to-all-start.1 = ((bf16[32,1,16,1024]{3,2,1,0:T(8,128)(2,1)}), bf16[32,1,16,1024]{3,2,1,0:T(8,128)(2,1)}, u32[]{:S(2)}, u32[]{:S(2)}) async-start(bf16[32,1,16,1024]{3,2,1,0:T(8,128)(2,1)} %bitcast.139), calls=%async_computation.1 | async-start | bytes 2097152 | tf_op jit(solution)/shard_map/all_to_all | solution.py:73
  101.5 101.0 %reduce-scatter.4.cloned.1.call-start = ((), (), s32[]{:S(2)}) async-start(), calls=%async_computation.8 | async-start | bytes 3342336
  102.5 2.9 copy-start.1
  105.3 1.7 copy-start.2
  107.1 10.6 %copy-start.8 = (f32[768]{0:T(1024)S(1)}, f32[768]{0:T(1024)}, u32[]{:S(2)}) copy-start(f32[768]{0:T(1024)} %broadcast_bitcast_fusion.1) | copy-start | bytes 9220
  107.1 10.6 %copy-start.11 = (bf16[1,768,1024]{2,1,0:T(8,128)(2,1)S(1)}, bf16[1,768,1024]{2,1,0:T(8,128)(2,1)}, u32[]{:S(2)}) copy-start(bf16[1,768,1024]{2,1,0:T(8,128)(2,1)} %param.14) | copy-start | bytes 4718596
  117.6 9.2 %slice-start = ((s8[6291456]{0:T(1024)(128)(4,1)}), s8[4194304]{0:T(1024)(128)(4,1)S(1)}, s32[]{:S(2)}) async-start(s8[6291456]{0:T(1024)(128)(4,1)} %bitcast.136), calls=%async_computation.9 | async-start | bytes 8388608
  122.9 3.8 %copy-start.15 = (bf16[32,16,768]{2,0,1:T(8,128)(2,1)}, bf16[32,16,768]{2,0,1:T(8,128)(2,1)S(1)}, u32[]{:S(2)}) copy-start(bf16[32,16,768]{2,0,1:T(8,128)(2,1)S(1)} %get-tuple-element.24) | copy-start | bytes 2359300
  122.9 3.8 %copy-start.16 = (bf16[32,16,768]{2,0,1:T(8,128)(2,1)}, bf16[32,16,768]{2,0,1:T(8,128)(2,1)S(1)}, u32[]{:S(2)}) copy-start(bf16[32,16,768]{2,0,1:T(8,128)(2,1)S(1)} %get-tuple-element.25) | copy-start | bytes 2359300
  123.0 3.9 %slice-start.1 = ((s8[6291456]{0:T(1024)(128)(4,1)}), s8[2097152]{0:T(1024)(128)(4,1)S(1)}, s32[]{:S(2)}) async-start(s8[6291456]{0:T(1024)(128)(4,1)} %bitcast.136), calls=%async_computation.10 | async-start | bytes 4194304
  131.6 1.4 copy-start.12
  131.6 1.6 copy-start.14
  135.8 22.0 %all-to-all-start.4 = ((bf16[32,1,16,1024]{3,2,1,0:T(8,128)(2,1)}), bf16[32,1,16,1024]{3,2,1,0:T(8,128)(2,1)}, u32[]{:S(2)}, u32[]{:S(2)}) async-start(bf16[32,1,16,1024]{3,2,1,0:T(8,128)(2,1)} %copy.86), calls=%async_computation.4 | async-start | bytes 2097152 | tf_op jit(solution)/shard_map/all_to_all | solution.py:102
  141.6 4.4 %copy-start.3 = (bf16[1024,1536,1]{0,1,2:T(8,128)(2,1)S(1)}, bf16[1024,1536,1]{0,1,2:T(8,128)(2,1)}, u32[]{:S(2)}) copy-start(bf16[1024,1536,1]{0,1,2:T(8,128)(2,1)} %copy-done.2) | copy-start | bytes 9437188
  141.6 203.2 %all-reduce.2.cloned.1.call-start = ((), (), s32[]{:S(2)}) async-start(), calls=%async_computation.7 | async-start | bytes 3145728 | tf_op jit(solution)/shard_map/psum | solution.py:118
  149.1 13.7 %copy-start.5 = (bf16[128,1024]{1,0:T(8,128)(2,1)S(1)}, bf16[128,1024]{1,0:T(8,128)(2,1)}, u32[]{:S(2)}) copy-start(bf16[128,1024]{1,0:T(8,128)(2,1)} %param.10) | copy-start | bytes 786436
  149.1 13.8 %copy-start.7 = (s32[128,2]{0,1:T(2,128)S(1)}, s32[128,2]{0,1:T(2,128)}, u32[]{:S(2)}) copy-start(s32[128,2]{0,1:T(2,128)} %copy-done.6) | copy-start | bytes 3076
  157.8 21.3 %all-to-all-start.3 = ((bf16[32,1,16,1024]{3,2,1,0:T(8,128)(2,1)}), bf16[32,1,16,1024]{3,2,1,0:T(8,128)(2,1)S(1)}, u32[]{:S(2)}, u32[]{:S(2)}) async-start(bf16[32,1,16,1024]{3,2,1,0:T(8,128)(2,1)} %copy.85), calls=%async_computation.3 | async-start | bytes 2097152 | tf_op jit(solution)/shard_map/all_to_all | solution.py:97
Sparse Core Ops, SparseCore 0:
  10.1 80.9 all-gather.1
  131.7 70.7 reduce-scatter.3
  205.4 139.2 all-reduce.1
where the time goes:
time: 355 us; the launch traced here: 354 us
  waiting for transfers between devices  250 us (70%)
  starting transfers between devices  33.6 us (9%)
  matrix products  29.9 us (8%)
  local copies, waits for them, and re-layouts  22.4 us (6%)
  between operations  14.1 us (4%)
  other arithmetic  4.22 us (1%)
    psum x1, waiting for transfers between devices, body(): down_grad = lax.psum(down_part.astype(jnp.bfloat16), 'dp')  140 us
    all_gather x1, waiting for transfers between devices, body(): gathered = lax.all_gather(gate_up_weight, 'dp', axis=0, tiled=True)  55.5 us
    unnamed x4, waiting for transfers between devices  23.1 us
    all_to_all x1, waiting for transfers between devices, body(): lax.all_to_all(row_grads, 'expert', split_axis=0, concat_axis=0, tiled=True)  13.8 us
    unnamed x45, local copies, waits for them, and re-layouts  13.5 us
    all_to_all x1, starting transfers between devices, body(): lax.all_to_all(send_probs, 'expert', split_axis=0, concat_axis=0, tiled=T...  9.4 us
    all_to_all x1, starting transfers between devices, body(): lax.all_to_all(send_grads, 'expert', split_axis=0, concat_axis=0, tiled=T...  7.21 us
    all_to_all x1, waiting for transfers between devices, body(): lax.all_to_all(expert_out.astype(jnp.bfloat16), 'expert', split_axis=0, c...  7.1 us
  transfers between devices with their start and end apart: 8, of which 7 were waited for; matrix products, arithmetic and copies ran while one was open for 10% of the time, Pallas kernels for 0%

commit v1 on v0

--- a/solution.py
+++ b/solution.py
@@ -77,7 +77,14 @@
     full_scale = jnp.repeat(level_rows, hidden, axis=2)
     down_scale = jnp.repeat(lookup(down_scale_index, scale_table), QBLOCK, axis=1)
     down_eff = (down_weight.astype(f32) * down_scale[:, :, None]).astype(jnp.bfloat16)
-    gathered = lax.all_gather(gate_up_weight, "dp", axis=0, tiled=True)
+    n_dev = lax.axis_size("dp")
+    route = [(i, (i + 1) % n_dev) for i in range(n_dev)]
+    blocks = [gate_up_weight]
+    for hop in range(1, n_dev):
+        blocks = [lax.ppermute(blocks[0], "dp", route), *blocks]
+    result = jnp.concatenate(blocks, axis=0)
+    shift = (lax.axis_index("dp") + 1) * blocks[-1].shape[0]
+    gathered = jnp.roll(result, shift, axis=0)
     gate_up_eff = (gathered.astype(f32) * full_scale).astype(jnp.bfloat16)
     projected = jnp.einsum("sjcd,djf->sjcf", recv_tokens, gate_up_eff, preferred_element_type=f32)
     gate_part = projected[..., :hidden]

time: 355 us -> 484 us (1.36)
  waiting for transfers between devices: 250 us -> 322 us
  starting transfers between devices: 33.6 us -> 64.4 us
  local copies, waits for them, and re-layouts: 22.4 us -> 41.3 us
    ppermute x0 -> x15, waiting for transfers between devices: none -> 136 us  [body(): blocks = [lax.ppermute(blocks[0], 'dp', route), *blocks]]
    all_gather x1 -> x0, waiting for transfers between devices: 55.5 us -> none  [body(): gathered = lax.all_gather(gate_up_weight, 'dp', axis=0, tiled=True)]
    ppermute x0 -> x15, starting transfers between devices: none -> 30.6 us  [body(): blocks = [lax.ppermute(blocks[0], 'dp', route), *blocks]]
    concatenate x0 -> x1, local copies, waits for them, and re-layouts: none -> 15.8 us  [body(): gathered = jnp.roll(result, shift, axis=0)]
    unnamed x45 -> x44, local copies, waits for them, and re-layouts: 13.5 us -> 19 us
    unnamed x4 -> x3, waiting for transfers between devices: 23.1 us -> 23 us
  transfers between devices with their start and end apart: 8 -> 22, of which waited for: 7 -> 19; matrix products, arithmetic and copies ran while one was open for 10% -> 12% of each run, Pallas kernels for 0% -> 0%
where the time goes in v1:
time: 484 us; the launch traced here: 481 us
  waiting for transfers between devices  322 us (67%)
  starting transfers between devices  64.4 us (13%)
  local copies, waits for them, and re-layouts  41.3 us (9%)
  matrix products  32.1 us (7%)
  between operations  14.5 us (3%)
  other arithmetic  7.1 us (1%)
    psum x1, waiting for transfers between devices, body(): down_grad = lax.psum(down_part.astype(jnp.bfloat16), 'dp')  140 us
    ppermute x15, waiting for transfers between devices, body(): blocks = [lax.ppermute(blocks[0], 'dp', route), *blocks]  136 us
    ppermute x15, starting transfers between devices, body(): blocks = [lax.ppermute(blocks[0], 'dp', route), *blocks]  30.6 us
    unnamed x3, waiting for transfers between devices  23 us
    unnamed x44, local copies, waits for them, and re-layouts  19 us
    concatenate x1, local copies, waits for them, and re-layouts, body(): gathered = jnp.roll(result, shift, axis=0)  15.8 us
    all_to_all x1, waiting for transfers between devices, body(): lax.all_to_all(row_grads, 'expert', split_axis=0, concat_axis=0, tiled=True)  13.8 us
  transfers between devices with their start and end apart: 22, of which 19 were waited for; matrix products, arithmetic and copies ran while one was open for 12% of the time, Pallas kernels for 0%

profile of v1, /device:TPU:2, one launch (start us, length us, event | category | flops | bytes accessed | tf_op | source)
XLA Modules:
  0.0 481.3 jit_solution(1390742933998654442)
XLA Ops:
  8.4 3.8 collective-permute-start
  12.2 16.7 %collective-permute-done = bf16[64,1,1536]{0,2,1:T(8,128)(2,1)S(1)} collective-permute-done((bf16[64,1,1536]{0,2,1:T(8,128)(2,1)S(1)}, bf16[64,1,1536]{0,2,1:T(8,128)(2,1)S(1)}, u32[]{:S(2)}, u32[]{:S(2)}) %collective-permute-start) | collective-permute-done | bytes 196640 | tf_op jit(solution)/shard_map/ppermute | solution.py:84
  28.9 1.9 collective-permute-start.1
  30.8 11.5 %collective-permute-done.1 = bf16[64,1,1536]{0,2,1:T(8,128)(2,1)S(1)} collective-permute-done((bf16[64,1,1536]{0,2,1:T(8,128)(2,1)S(1)}, bf16[64,1,1536]{0,2,1:T(8,128)(2,1)S(1)}, u32[]{:S(2)}, u32[]{:S(2)}) %collective-permute-start.1) | collective-permute-done | bytes 196640 | tf_op jit(solution)/shard_map/ppermute | solution.py:84
  42.3 1.9 collective-permute-start.2
  44.2 10.6 %collective-permute-done.2 = bf16[64,1,1536]{0,2,1:T(8,128)(2,1)S(1)} collective-permute-done((bf16[64,1,1536]{0,2,1:T(8,128)(2,1)S(1)}, bf16[64,1,1536]{0,2,1:T(8,128)(2,1)S(1)}, u32[]{:S(2)}, u32[]{:S(2)}) %collective-permute-start.2) | collective-permute-done | bytes 196640 | tf_op jit(solution)/shard_map/ppermute | solution.py:84
  56.7 9.6 %collective-permute-done.3 = bf16[64,1,1536]{0,2,1:T(8,128)(2,1)S(1)} collective-permute-done((bf16[64,1,1536]{0,2,1:T(8,128)(2,1)S(1)}, bf16[64,1,1536]{0,2,1:T(8,128)(2,1)S(1)}, u32[]{:S(2)}, u32[]{:S(2)}) %collective-permute-start.3) | collective-permute-done | bytes 196640 | tf_op jit(solution)/shard_map/ppermute | solution.py:84
  66.3 1.9 collective-permute-start.4
  68.2 9.0 %collective-permute-done.4 = bf16[64,1,1536]{0,2,1:T(8,128)(2,1)S(1)} collective-permute-done((bf16[64,1,1536]{0,2,1:T(8,128)(2,1)S(1)}, bf16[64,1,1536]{0,2,1:T(8,128)(2,1)S(1)}, u32[]{:S(2)}, u32[]{:S(2)}) %collective-permute-start.4) | collective-permute-done | bytes 196640 | tf_op jit(solution)/shard_map/ppermute | solution.py:84
  77.2 1.9 collective-permute-start.5
  79.1 9.0 %collective-permute-done.5 = bf16[64,1,1536]{0,2,1:T(8,128)(2,1)S(1)} collective-permute-done((bf16[64,1,1536]{0,2,1:T(8,128)(2,1)S(1)}, bf16[64,1,1536]{0,2,1:T(8,128)(2,1)S(1)}, u32[]{:S(2)}, u32[]{:S(2)}) %collective-permute-start.5) | collective-permute-done | bytes 196640 | tf_op jit(solution)/shard_map/ppermute | solution.py:84
  91.3 8.7 %collective-permute-done.6 = bf16[64,1,1536]{0,2,1:T(8,128)(2,1)S(1)} collective-permute-done((bf16[64,1,1536]{0,2,1:T(8,128)(2,1)S(1)}, bf16[64,1,1536]{0,2,1:T(8,128)(2,1)S(1)}, u32[]{:S(2)}, u32[]{:S(2)}) %collective-permute-start.6) | collective-permute-done | bytes 196640 | tf_op jit(solution)/shard_map/ppermute | solution.py:84
  100.0 1.9 collective-permute-start.7
  102.7 10.2 %collective-permute-done.7 = bf16[64,1,1536]{0,2,1:T(8,128)(2,1)} collective-permute-done((bf16[64,1,1536]{0,2,1:T(8,128)(2,1)S(1)}, bf16[64,1,1536]{0,2,1:T(8,128)(2,1)}, u32[]{:S(2)}, u32[]{:S(2)}) %collective-permute-start.7) | collective-permute-done | bytes 196640 | tf_op jit(solution)/shard_map/ppermute | solution.py:84
  112.9 1.9 collective-permute-start.8
  116.4 7.6 %all-to-all-start = ((bf16[32,1,16]{2,1,0:T(2,128)(2,1)}), bf16[32,1,16]{2,1,0:T(2,128)(2,1)S(1)}, u32[]{:S(2)}, u32[]{:S(2)}) async-start(bf16[32,1,16]{2,1,0:T(2,128)(2,1)} %reshape.246), calls=%async_computation | async-start | bytes 32768 | tf_op jit(solution)/shard_map/all_to_all | solution.py:74
  124.1 1.9 collective-permute-start.9
  126.1 12.7 %collective-permute-done.9 = bf16[64,1,1536]{0,2,1:T(8,128)(2,1)S(1)} collective-permute-done((bf16[64,1,1536]{0,2,1:T(8,128)(2,1)}, bf16[64,1,1536]{0,2,1:T(8,128)(2,1)S(1)}, u32[]{:S(2)}, u32[]{:S(2)}) %collective-permute-start.9) | collective-permute-done | bytes 196640 | tf_op jit(solution)/shard_map/ppermute | solution.py:84
  138.8 1.9 collective-permute-start.10
  140.8 11.9 %collective-permute-done.10 = bf16[64,1,1536]{0,2,1:T(8,128)(2,1)} collective-permute-done((bf16[64,1,1536]{0,2,1:T(8,128)(2,1)S(1)}, bf16[64,1,1536]{0,2,1:T(8,128)(2,1)}, u32[]{:S(2)}, u32[]{:S(2)}) %collective-permute-start.10) | collective-permute-done | bytes 196640 | tf_op jit(solution)/shard_map/ppermute | solution.py:84
  152.7 1.9 collective-permute-start.11
  156.1 7.2 %all-to-all-start.2 = ((bf16[32,1,16,1024]{3,2,1,0:T(8,128)(2,1)}), bf16[32,1,16,1024]{3,2,1,0:T(8,128)(2,1)}, u32[]{:S(2)}, u32[]{:S(2)}) async-start(bf16[32,1,16,1024]{3,2,1,0:T(8,128)(2,1)} %bitcast.19), calls=%async_computation.2 | async-start | bytes 2097152 | tf_op jit(solution)/shard_map/all_to_all | solution.py:72
  165.9 1.9 collective-permute-start.12
  170.6 8.3 %collective-permute-done.12 = bf16[64,1,1536]{0,2,1:T(8,128)(2,1)} collective-permute-done((bf16[64,1,1536]{0,2,1:T(8,128)(2,1)}, bf16[64,1,1536]{0,2,1:T(8,128)(2,1)}, u32[]{:S(2)}, u32[]{:S(2)}) %collective-permute-start.12) | collective-permute-done | bytes 196640 | tf_op jit(solution)/shard_map/ppermute | solution.py:84
  179.0 1.9 collective-permute-start.13
  180.9 2.4 convolution_convert_fusion.2
  183.3 8.2 %collective-permute-done.13 = bf16[64,1,1536]{0,2,1:T(8,128)(2,1)} collective-permute-done((bf16[64,1,1536]{0,2,1:T(8,128)(2,1)}, bf16[64,1,1536]{0,2,1:T(8,128)(2,1)}, u32[]{:S(2)}, u32[]{:S(2)}) %collective-permute-start.13) | collective-permute-done | bytes 196640 | tf_op jit(solution)/shard_map/ppermute | solution.py:84
  191.5 1.9 collective-permute-start.14
  195.5 7.6 %collective-permute-done.14 = bf16[64,1,1536]{0,2,1:T(8,128)(2,1)} collective-permute-done((bf16[64,1,1536]{0,2,1:T(8,128)(2,1)}, bf16[64,1,1536]{0,2,1:T(8,128)(2,1)}, u32[]{:S(2)}, u32[]{:S(2)}) %collective-permute-start.14) | collective-permute-done | bytes 196640 | tf_op jit(solution)/shard_map/ppermute | solution.py:84
  203.1 15.8 %concatenate.18 = bf16[2048,1,1536]{0,2,1:T(8,128)(2,1)} concatenate(bf16[64,1,1536]{0,2,1:T(8,128)(2,1)} %collective-permute-done.14, bf16[64,1,1536]{0,2,1:T(8,128)(2,1)} %collective-permute-done.13, bf16[64,1,1536]{0,2,1:T(8,128)(2,1)} %collective-permute-done.12, bf16[64,1,1536]{0,2,1:T(8,128)(2,1)} %collective-permute-done.11, bf16[64,1,1536]{0,2,1:T(8,128)(2,1)} %collective-permute-done.10, ...), dimensions={0} | concatenate | bytes 12582912 | tf_op jit(solution)/shard_map/jit(_roll_dynamic)/concatenate | solution.py:87
  219.0 7.8 %all-to-all-start.1 = ((bf16[32,1,16,1024]{3,2,1,0:T(8,128)(2,1)}), bf16[32,1,16,1024]{3,2,1,0:T(8,128)(2,1)S(1)}, u32[]{:S(2)}, u32[]{:S(2)}) async-start(bf16[32,1,16,1024]{3,2,1,0:T(8,128)(2,1)} %bitcast.13), calls=%async_computation.1 | async-start | bytes 2097152 | tf_op jit(solution)/shard_map/all_to_all | solution.py:73
  227.8 4.2 copy-done.2
  232.1 2.1 fusion.3
  235.9 5.3 %convolution_bitcast_fusion = f32[32,1,16,1536]{3,0,2,1:T(8,128)} fusion(bf16[1024,1536,1]{0,1,2:T(8,128)(2,1)S(1)} %fusion.3, bf16[32,1,16,1024]{3,2,1,0:T(8,128)(2,1)} %all-to-all-done.2), kind=kOutput, calls=%fused_computation.4 | convolution fusion | flops 1610612736 | bytes 7340032 | tf_op jit(solution)/shard_map/sjcd,djf->sjcf/dot_general | solution.py:89
  242.9 5.3 %fusion.31 = (bf16[32,16,768]{2,0,1:T(8,128)(2,1)S(1)}, bf16[32,16,768]{2,0,1:T(8,128)(2,1)S(1)}, bf16[32,1,16,768]{3,0,2,1:T(8,128)(2,1)}) fusion(f32[32,1,16,1536]{3,0,2,1:T(8,128)} %convolution_bitcast_fusion, bf16[32,1,16,1024]{3,2,1,0:T(8,128)(2,1)S(1)} %all-to-all-done.1, bf16[1,768,1024]{2,1,0:T(8,128)(2,1)S(1)} %copy-done.12, ...), kind=kOutput, calls=%fused_computation.49 | convolution fusion | flops 813957120 | bytes 8131584 | tf_op jit(solution)/shard_map/sjcd,jfd->sjcf/dot_general | solution.py:95
  248.2 3.8 fusion.17
  253.8 3.0 copy.106
  258.2 2.2 fusion.12
  262.0 5.8 %all-to-all-start.4 = ((bf16[32,1,16,1024]{3,2,1,0:T(8,128)(2,1)}), bf16[32,1,16,1024]{3,2,1,0:T(8,128)(2,1)}, u32[]{:S(2)}, u32[]{:S(2)}) async-start(bf16[32,1,16,1024]{3,2,1,0:T(8,128)(2,1)} %copy.96), calls=%async_computation.4 | async-start | bytes 2097152 | tf_op jit(solution)/shard_map/all_to_all | solution.py:109
  268.1 4.0 fusion.11
  272.2 3.2 fusion.13
  276.9 7.1 %all-to-all-done.4 = bf16[32,1,16,1024]{3,2,1,0:T(8,128)(2,1)} async-done(((bf16[32,1,16,1024]{3,2,1,0:T(8,128)(2,1)}), bf16[32,1,16,1024]{3,2,1,0:T(8,128)(2,1)}, u32[]{:S(2)}, u32[]{:S(2)}) %all-to-all-start.4) | async-done | bytes 1048608 | tf_op jit(solution)/shard_map/all_to_all | solution.py:109
  284.0 5.0 %all-to-all-start.3 = ((bf16[32,1,16,1024]{3,2,1,0:T(8,128)(2,1)}), bf16[32,1,16,1024]{3,2,1,0:T(8,128)(2,1)S(1)}, u32[]{:S(2)}, u32[]{:S(2)}) async-start(bf16[32,1,16,1024]{3,2,1,0:T(8,128)(2,1)} %copy.95), calls=%async_computation.3 | async-start | bytes 2097152 | tf_op jit(solution)/shard_map/all_to_all | solution.py:104
  289.1 2.4 fusion.14
  291.5 13.8 %all-to-all-done.3 = bf16[32,1,16,1024]{3,2,1,0:T(8,128)(2,1)S(1)} async-done(((bf16[32,1,16,1024]{3,2,1,0:T(8,128)(2,1)}), bf16[32,1,16,1024]{3,2,1,0:T(8,128)(2,1)S(1)}, u32[]{:S(2)}, u32[]{:S(2)}) %all-to-all-start.3) | async-done | bytes 1048608 | tf_op jit(solution)/shard_map/all_to_all | solution.py:104
  306.3 23.0 %reduce-scatter.4.cloned.1.call-done = bf16[64,1536]{1,0:T(8,128)(2,1)} async-done(((bf16[1024,1536]{1,0:T(8,128)(2,1)}), bf16[64,1536]{1,0:T(8,128)(2,1)}) %reduce-scatter.4.cloned.1.call-update) | async-done | bytes 196624
  331.3 140.5 %all-reduce.2.cloned.1.call-done = bf16[1,768,1024]{2,1,0:T(8,128)(2,1)} async-done(((bf16[1,768,1024]{2,1,0:T(8,128)(2,1)}), bf16[1,768,1024]{2,1,0:T(8,128)(2,1)}) %all-reduce.2.cloned.1.call-update) | async-done | bytes 1572880 | tf_op jit(solution)/shard_map/psum | solution.py:125
  471.8 2.7 copy.132
  (75 shorter events, 31.8 us)
Async XLA Ops:
  7.2 147.5 %copy-start = (bf16[128,1024]{1,0:T(8,128)(2,1)S(1)}, bf16[128,1024]{1,0:T(8,128)(2,1)}, u32[]{:S(2)}) copy-start(bf16[128,1024]{1,0:T(8,128)(2,1)} %param.9) | copy-start | bytes 786436
  8.4 20.5 %collective-permute-start = (bf16[64,1,1536]{0,2,1:T(8,128)(2,1)S(1)}, bf16[64,1,1536]{0,2,1:T(8,128)(2,1)S(1)}, u32[]{:S(2)}, u32[]{:S(2)}) collective-permute-start(bf16[64,1,1536]{0,2,1:T(8,128)(2,1)S(1)} %copy.84), channel_id=1, source_target_pairs={{0,32},{32,64},{64,96},{96,128},{128,160},{160,192},{192,224},{224... | collective-permute-start | bytes 589832 | tf_op jit(solution)/shard_map/ppermute | solution.py:84
  28.9 13.4 %collective-permute-start.1 = (bf16[64,1,1536]{0,2,1:T(8,128)(2,1)S(1)}, bf16[64,1,1536]{0,2,1:T(8,128)(2,1)S(1)}, u32[]{:S(2)}, u32[]{:S(2)}) collective-permute-start(bf16[64,1,1536]{0,2,1:T(8,128)(2,1)S(1)} %collective-permute-done), channel_id=1, source_target_pairs={{0,32},{32,64},{64,96},{96,128},{128,160},{160,192},{192,224},{224... | collective-permute-start | bytes 589832 | tf_op jit(solution)/shard_map/ppermute | solution.py:84
  42.3 12.5 %collective-permute-start.2 = (bf16[64,1,1536]{0,2,1:T(8,128)(2,1)S(1)}, bf16[64,1,1536]{0,2,1:T(8,128)(2,1)S(1)}, u32[]{:S(2)}, u32[]{:S(2)}) collective-permute-start(bf16[64,1,1536]{0,2,1:T(8,128)(2,1)S(1)} %collective-permute-done.1), channel_id=1, source_target_pairs={{0,32},{32,64},{64,96},{96,128},{128,160},{160,192},{192,224},{224... | collective-permute-start | bytes 589832 | tf_op jit(solution)/shard_map/ppermute | solution.py:84
  54.8 11.6 %collective-permute-start.3 = (bf16[64,1,1536]{0,2,1:T(8,128)(2,1)S(1)}, bf16[64,1,1536]{0,2,1:T(8,128)(2,1)S(1)}, u32[]{:S(2)}, u32[]{:S(2)}) collective-permute-start(bf16[64,1,1536]{0,2,1:T(8,128)(2,1)S(1)} %collective-permute-done.2), channel_id=1, source_target_pairs={{0,32},{32,64},{64,96},{96,128},{128,160},{160,192},{192,224},{224... | collective-permute-start | bytes 589832 | tf_op jit(solution)/shard_map/ppermute | solution.py:84
  66.3 10.9 %collective-permute-start.4 = (bf16[64,1,1536]{0,2,1:T(8,128)(2,1)S(1)}, bf16[64,1,1536]{0,2,1:T(8,128)(2,1)S(1)}, u32[]{:S(2)}, u32[]{:S(2)}) collective-permute-start(bf16[64,1,1536]{0,2,1:T(8,128)(2,1)S(1)} %collective-permute-done.3), channel_id=1, source_target_pairs={{0,32},{32,64},{64,96},{96,128},{128,160},{160,192},{192,224},{224... | collective-permute-start | bytes 589832 | tf_op jit(solution)/shard_map/ppermute | solution.py:84
  77.2 10.9 %collective-permute-start.5 = (bf16[64,1,1536]{0,2,1:T(8,128)(2,1)S(1)}, bf16[64,1,1536]{0,2,1:T(8,128)(2,1)S(1)}, u32[]{:S(2)}, u32[]{:S(2)}) collective-permute-start(bf16[64,1,1536]{0,2,1:T(8,128)(2,1)S(1)} %collective-permute-done.4), channel_id=1, source_target_pairs={{0,32},{32,64},{64,96},{96,128},{128,160},{160,192},{192,224},{224... | collective-permute-start | bytes 589832 | tf_op jit(solution)/shard_map/ppermute | solution.py:84
  88.1 12.0 %collective-permute-start.6 = (bf16[64,1,1536]{0,2,1:T(8,128)(2,1)S(1)}, bf16[64,1,1536]{0,2,1:T(8,128)(2,1)S(1)}, u32[]{:S(2)}, u32[]{:S(2)}) collective-permute-start(bf16[64,1,1536]{0,2,1:T(8,128)(2,1)S(1)} %collective-permute-done.5), channel_id=1, source_target_pairs={{0,32},{32,64},{64,96},{96,128},{128,160},{160,192},{192,224},{224... | collective-permute-start | bytes 589832 | tf_op jit(solution)/shard_map/ppermute | solution.py:84
  100.0 12.8 %collective-permute-start.7 = (bf16[64,1,1536]{0,2,1:T(8,128)(2,1)S(1)}, bf16[64,1,1536]{0,2,1:T(8,128)(2,1)}, u32[]{:S(2)}, u32[]{:S(2)}) collective-permute-start(bf16[64,1,1536]{0,2,1:T(8,128)(2,1)S(1)} %collective-permute-done.6), channel_id=1, source_target_pairs={{0,32},{32,64},{64,96},{96,128},{128,160},{160,192},{192,224},{224... | collective-permute-start | bytes 589832 | tf_op jit(solution)/shard_map/ppermute | solution.py:84
  102.7 36.2 %copy-start.9 = (s32[128,2]{0,1:T(2,128)}, s32[128,2]{0,1:T(2,128)S(1)}, u32[]{:S(2)}) copy-start(s32[128,2]{0,1:T(2,128)S(1)} %multiply_add_fusion) | copy-start | bytes 3076
  112.9 11.2 %collective-permute-start.8 = (bf16[64,1,1536]{0,2,1:T(8,128)(2,1)}, bf16[64,1,1536]{0,2,1:T(8,128)(2,1)}, u32[]{:S(2)}, u32[]{:S(2)}) collective-permute-start(bf16[64,1,1536]{0,2,1:T(8,128)(2,1)} %collective-permute-done.7), channel_id=1, source_target_pairs={{0,32},{32,64},{64,96},{96,128},{128,160},{160,192},{192,224},{224... | collective-permute-start | bytes 589832 | tf_op jit(solution)/shard_map/ppermute | solution.py:84
  116.4 39.6 %all-to-all-start = ((bf16[32,1,16]{2,1,0:T(2,128)(2,1)}), bf16[32,1,16]{2,1,0:T(2,128)(2,1)S(1)}, u32[]{:S(2)}, u32[]{:S(2)}) async-start(bf16[32,1,16]{2,1,0:T(2,128)(2,1)} %reshape.246), calls=%async_computation | async-start | bytes 32768 | tf_op jit(solution)/shard_map/all_to_all | solution.py:74
  124.1 14.8 %collective-permute-start.9 = (bf16[64,1,1536]{0,2,1:T(8,128)(2,1)}, bf16[64,1,1536]{0,2,1:T(8,128)(2,1)S(1)}, u32[]{:S(2)}, u32[]{:S(2)}) collective-permute-start(bf16[64,1,1536]{0,2,1:T(8,128)(2,1)} %collective-permute-done.8), channel_id=1, source_target_pairs={{0,32},{32,64},{64,96},{96,128},{128,160},{160,192},{192,224},{224... | collective-permute-start | bytes 589832 | tf_op jit(solution)/shard_map/ppermute | solution.py:84
  138.8 2.0 copy-start.5
  138.8 13.9 %collective-permute-start.10 = (bf16[64,1,1536]{0,2,1:T(8,128)(2,1)S(1)}, bf16[64,1,1536]{0,2,1:T(8,128)(2,1)}, u32[]{:S(2)}, u32[]{:S(2)}) collective-permute-start(bf16[64,1,1536]{0,2,1:T(8,128)(2,1)S(1)} %collective-permute-done.9), channel_id=1, source_target_pairs={{0,32},{32,64},{64,96},{96,128},{128,160},{160,192},{192,224},{224... | collective-permute-start | bytes 589832 | tf_op jit(solution)/shard_map/ppermute | solution.py:84
  152.7 13.2 %collective-permute-start.11 = (bf16[64,1,1536]{0,2,1:T(8,128)(2,1)}, bf16[64,1,1536]{0,2,1:T(8,128)(2,1)}, u32[]{:S(2)}, u32[]{:S(2)}) collective-permute-start(bf16[64,1,1536]{0,2,1:T(8,128)(2,1)} %collective-permute-done.10), channel_id=1, source_target_pairs={{0,32},{32,64},{64,96},{96,128},{128,160},{160,192},{192,224},{224... | collective-permute-start | bytes 589832 | tf_op jit(solution)/shard_map/ppermute | solution.py:84
  156.1 62.9 %all-to-all-start.2 = ((bf16[32,1,16,1024]{3,2,1,0:T(8,128)(2,1)}), bf16[32,1,16,1024]{3,2,1,0:T(8,128)(2,1)}, u32[]{:S(2)}, u32[]{:S(2)}) async-start(bf16[32,1,16,1024]{3,2,1,0:T(8,128)(2,1)} %bitcast.19), calls=%async_computation.2 | async-start | bytes 2097152 | tf_op jit(solution)/shard_map/all_to_all | solution.py:72
  165.9 13.1 %collective-permute-start.12 = (bf16[64,1,1536]{0,2,1:T(8,128)(2,1)}, bf16[64,1,1536]{0,2,1:T(8,128)(2,1)}, u32[]{:S(2)}, u32[]{:S(2)}) collective-permute-start(bf16[64,1,1536]{0,2,1:T(8,128)(2,1)} %collective-permute-done.11), channel_id=1, source_target_pairs={{0,32},{32,64},{64,96},{96,128},{128,160},{160,192},{192,224},{224... | collective-permute-start | bytes 589832 | tf_op jit(solution)/shard_map/ppermute | solution.py:84
  179.0 12.5 %collective-permute-start.13 = (bf16[64,1,1536]{0,2,1:T(8,128)(2,1)}, bf16[64,1,1536]{0,2,1:T(8,128)(2,1)}, u32[]{:S(2)}, u32[]{:S(2)}) collective-permute-start(bf16[64,1,1536]{0,2,1:T(8,128)(2,1)} %collective-permute-done.12), channel_id=1, source_target_pairs={{0,32},{32,64},{64,96},{96,128},{128,160},{160,192},{192,224},{224... | collective-permute-start | bytes 589832 | tf_op jit(solution)/shard_map/ppermute | solution.py:84
  191.5 11.6 %collective-permute-start.14 = (bf16[64,1,1536]{0,2,1:T(8,128)(2,1)}, bf16[64,1,1536]{0,2,1:T(8,128)(2,1)}, u32[]{:S(2)}, u32[]{:S(2)}) collective-permute-start(bf16[64,1,1536]{0,2,1:T(8,128)(2,1)} %collective-permute-done.13), channel_id=1, source_target_pairs={{0,32},{32,64},{64,96},{96,128},{128,160},{160,192},{192,224},{224... | collective-permute-start | bytes 589832 | tf_op jit(solution)/shard_map/ppermute | solution.py:84
  219.0 8.0 %copy-start.8 = (f32[1,2,8,128]{3,1,2,0:T(2,128)S(1)}, f32[1,2,8,128]{3,1,2,0:T(2,128)}, u32[]{:S(2)}) copy-start(f32[1,2,8,128]{3,1,2,0:T(2,128)} %copy.130) | copy-start | bytes 24580
  219.0 23.9 %all-to-all-start.1 = ((bf16[32,1,16,1024]{3,2,1,0:T(8,128)(2,1)}), bf16[32,1,16,1024]{3,2,1,0:T(8,128)(2,1)S(1)}, u32[]{:S(2)}, u32[]{:S(2)}) async-start(bf16[32,1,16,1024]{3,2,1,0:T(8,128)(2,1)} %bitcast.13), calls=%async_computation.1 | async-start | bytes 2097152 | tf_op jit(solution)/shard_map/all_to_all | solution.py:73
  226.8 102.5 %reduce-scatter.4.cloned.1.call-start = ((), (), s32[]{:S(2)}) async-start(), calls=%async_computation.7 | async-start | bytes 3342336
  227.0 5.1 %copy-start.2 = (bf16[2048,1,1536]{0,2,1:T(8,128)(2,1)S(1)}, bf16[2048,1,1536]{0,2,1:T(8,128)(2,1)}, u32[]{:S(2)}) copy-start(bf16[2048,1,1536]{0,2,1:T(8,128)(2,1)} %concatenate.18) | copy-start | bytes 18874372
  227.8 6.4 %copy-start.1 = (f32[1024,2,768]{0,2,1:T(8,128)}, f32[1024,2,768]{0,2,1:T(8,128)S(1)}, u32[]{:S(2)}) copy-start(f32[1024,2,768]{0,2,1:T(8,128)S(1)} %broadcast_in_dim.14) | copy-start | bytes 18874372
  234.2 1.7 copy-start.3
  235.9 6.9 %copy-start.11 = (f32[768]{0:T(1024)S(1)}, f32[768]{0:T(1024)}, u32[]{:S(2)}) copy-start(f32[768]{0:T(1024)} %broadcast_bitcast_fusion.1) | copy-start | bytes 9220
  235.9 6.9 %copy-start.12 = (bf16[1,768,1024]{2,1,0:T(8,128)(2,1)S(1)}, bf16[1,768,1024]{2,1,0:T(8,128)(2,1)}, u32[]{:S(2)}) copy-start(bf16[1,768,1024]{2,1,0:T(8,128)(2,1)} %param.14) | copy-start | bytes 4718596
  242.9 5.3 %copy-start.6 = (bf16[32,1,16,1024]{3,2,1,0:T(8,128)(2,1)}, bf16[32,1,16,1024]{3,2,1,0:T(8,128)(2,1)S(1)}, u32[]{:S(2)}) copy-start(bf16[32,1,16,1024]{3,2,1,0:T(8,128)(2,1)S(1)} %all-to-all-done.1) | copy-start | bytes 3145732
  242.9 9.2 %slice-start = ((s8[6291456]{0:T(1024)(128)(4,1)}), s8[4194304]{0:T(1024)(128)(4,1)S(1)}, s32[]{:S(2)}) async-start(s8[6291456]{0:T(1024)(128)(4,1)} %bitcast.136), calls=%async_computation.8 | async-start | bytes 8388608
  248.2 3.9 copy-start.14
  248.2 3.9 copy-start.15
  248.2 3.9 slice-start.1
  256.8 1.4 copy-start.13
  262.0 22.0 %all-to-all-start.4 = ((bf16[32,1,16,1024]{3,2,1,0:T(8,128)(2,1)}), bf16[32,1,16,1024]{3,2,1,0:T(8,128)(2,1)}, u32[]{:S(2)}, u32[]{:S(2)}) async-start(bf16[32,1,16,1024]{3,2,1,0:T(8,128)(2,1)} %copy.96), calls=%async_computation.4 | async-start | bytes 2097152 | tf_op jit(solution)/shard_map/all_to_all | solution.py:109
  267.8 4.3 copy-start.4
  267.8 204.0 %all-reduce.2.cloned.1.call-start = ((), (), s32[]{:S(2)}) async-start(), calls=%async_computation.6 | async-start | bytes 3145728 | tf_op jit(solution)/shard_map/psum | solution.py:125
  275.3 13.7 %copy-start.7 = (bf16[128,1024]{1,0:T(8,128)(2,1)S(1)}, bf16[128,1024]{1,0:T(8,128)(2,1)}, u32[]{:S(2)}) copy-start(bf16[128,1024]{1,0:T(8,128)(2,1)} %param.10) | copy-start | bytes 786436
  275.3 13.8 %copy-start.10 = (s32[128,2]{0,1:T(2,128)S(1)}, s32[128,2]{0,1:T(2,128)}, u32[]{:S(2)}) copy-start(s32[128,2]{0,1:T(2,128)} %copy-done.9) | copy-start | bytes 3076
  284.0 21.3 %all-to-all-start.3 = ((bf16[32,1,16,1024]{3,2,1,0:T(8,128)(2,1)}), bf16[32,1,16,1024]{3,2,1,0:T(8,128)(2,1)S(1)}, u32[]{:S(2)}, u32[]{:S(2)}) async-start(bf16[32,1,16,1024]{3,2,1,0:T(8,128)(2,1)} %copy.95), calls=%async_computation.3 | async-start | bytes 2097152 | tf_op jit(solution)/shard_map/all_to_all | solution.py:104
Sparse Core Ops, SparseCore 0:
  257.0 72.2 reduce-scatter.3
  332.2 139.5 all-reduce.1
